TPU v7x, 512 devices: a whole 4x4x16 slice. The times are simulated.
512 devices in a mesh: fsdp: 32 (over z, core), tensor: 16 (over y, x).
Axes of the slice: x: 4, y: 4, z: 16, core: 2. Of those that a mesh axis runs over, the one named last changes fastest.
Arguments:
- hidden: bfloat16 [4096, 14336], P('fsdp', 'tensor'), may hold values from -6 to 6
- grad_out: bfloat16 [4096, 4096], P('fsdp', 'tensor'), may hold values from -6 to 6
- weight_slots: bfloat16 [16, 512, 4096], P('tensor', 'fsdp'), may hold values from -0.09375 to 0.09375
- block_ids: int32 [16, 512], P('tensor', 'fsdp'), may hold values from 0 to 895, as said below
- slot_count: int32 [16, 32], P('tensor', 'fsdp'), may hold values from 2 to 16, as said below
Outputs:
- projected: bfloat16 [4096, 4096], P('fsdp', 'tensor')
- d_hidden: bfloat16 [4096, 14336], P('fsdp', 'tensor')
- grad_slots: float32 [16, 512, 4096], P('tensor', 'fsdp')
Inputs may be any that keep to these rules, and one draw needn't show every extreme that they name: `block_ids`: entry k of tensor shard s names the block at block row r and block column c of that shard's 14 x 64 grid as r * 64 + c; the 512 entries of one shard are all distinct; entries j * 16 to j * 16 + 15 are the slots stored by fsdp index j. The first slot_count[s, j] slots of fsdp index j in tensor shard s hold kept blocks; its other slots are empty.
All inputs are finite; a program needn't handle non-finite values.
Results may differ from a plain program's by a relative error of at most 0.018.
Values may be sent and summed in bfloat16 or wider, within the bound.
A program may use at most 128 MiB of HBM per device.

v0:
```python
import math

import jax
import jax.numpy as jnp
from jax import lax
from jax.sharding import PartitionSpec as P

BLK = 64


def build_window(slot_blocks, block_index, block_rows, block_cols):
    block_grid = (
        jnp.zeros((block_rows * block_cols, BLK * BLK), slot_blocks.dtype)
        .at[block_index]
        .set(slot_blocks)
    )
    block_grid = block_grid.reshape(block_rows, block_cols, BLK, BLK).transpose(0, 2, 1, 3)
    return block_grid.reshape(block_rows * BLK, block_cols * BLK)


def on_device(hidden, grad_out, weight_slots, block_ids, slot_count):
    tok_rows, unit_count = hidden.shape
    capacity = weight_slots.shape[1]
    block_rows = unit_count // BLK
    owners = lax.axis_size("fsdp")
    block_cols = grad_out.shape[1] * lax.axis_size("tensor") // BLK
    own_live = jnp.arange(capacity) < slot_count[0, 0]
    masked = jnp.where(own_live[None, :, None], weight_slots, jnp.zeros_like(weight_slots))
    gathered = (
        lax.all_gather(masked, "fsdp", axis=1, tiled=True),
        lax.all_gather(block_ids, "fsdp", axis=1, tiled=True),
    )
    slot_blocks = gathered[0][0]
    block_index = gathered[1][0]
    window_dense = build_window(slot_blocks, block_index, block_rows, block_cols)
    partial_value = jnp.dot(hidden, window_dense, preferred_element_type=jnp.float32)
    projected = lax.psum_scatter(
        partial_value.astype(jnp.bfloat16), "tensor", scatter_dimension=1, tiled=True
    )
    full_grad = lax.all_gather(grad_out, "tensor", axis=1, tiled=True)
    grad_columns = full_grad.reshape(tok_rows, block_cols, BLK)
    piece_blocks = lax.all_gather(masked, "fsdp", axis=1, tiled=True)[0]
    piece_index = lax.all_gather(block_ids, "fsdp", axis=1, tiled=True)[0]
    piece_count = piece_index.shape[0]
    selected = jnp.take(grad_columns, piece_index % block_cols, axis=1)
    piece_weights = piece_blocks.reshape(piece_count, BLK, BLK)
    row_terms = jnp.einsum(
        "tnj,nij->nti", selected, piece_weights, preferred_element_type=jnp.float32
    )
    folded = jax.ops.segment_sum(row_terms, piece_index // block_cols, num_segments=block_rows)
    d_hidden = folded.transpose(1, 0, 2).reshape(tok_rows, unit_count).astype(jnp.bfloat16)
    product = jnp.einsum("tr,td->rd", hidden, full_grad, preferred_element_type=jnp.float32).astype(
        jnp.bfloat16
    )
    picked = product.reshape(block_rows, BLK, block_cols, BLK)[
        block_index // block_cols, :, block_index % block_cols, :
    ]
    outgoing = picked.reshape(owners, capacity, BLK * BLK)
    incoming = lax.all_to_all(outgoing, "fsdp", split_axis=0, concat_axis=0, tiled=True)
    summed_grad = jnp.sum(incoming.astype(jnp.float32), axis=0)
    grad_scale = 1.0 / math.sqrt(tok_rows * owners)
    grad_blocks = jnp.where(
        own_live[:, None], summed_grad * grad_scale, jnp.zeros_like(summed_grad)
    )
    return (projected, d_hidden, grad_blocks[None])


def solution(mesh):
    in_specs = (
        P("fsdp", "tensor"),
        P("fsdp", "tensor"),
        P("tensor", "fsdp", None),
        P("tensor", "fsdp"),
        P("tensor", "fsdp"),
    )
    out_specs = (P("fsdp", "tensor"), P("fsdp", "tensor"), P("tensor", "fsdp", None))
    return jax.shard_map(
        on_device, mesh=mesh, in_specs=in_specs, out_specs=out_specs, check_vma=False
    )
```

profile of v0, /device:TPU:33, one launch (start us, length us, event | category | flops | bytes accessed | tf_op | source)
XLA Modules:
  0.0 502.1 jit_solution(9076358260025627654)
XLA Ops:
  8.1 1.6 copy.27
  9.7 1.3 dynamic-slice
  12.4 22.7 %all-reduce = s32[512]{0:T(512)S(1)} all-reduce(s32[512]{0:T(512)S(1)} %bitcast_dynamic-update-slice_fusion), channel_id=1, replica_groups=mesh['fsdp'=32,'tensor'=16] {'fsdp'}, use_global_device_ids=true, to_apply=%add | all-reduce | flops 512 | bytes 4096 | tf_op jit(solution)/shard_map/squeeze | solution.py:34
  35.1 38.0 %all-gather.5.cloned.1.call-done = bf16[128,4096]{0,1:T(8,128)(2,1)} async-done(((bf16[128,256]{0,1:T(8,128)(2,1)}), bf16[128,4096]{0,1:T(8,128)(2,1)}) %all-gather.5.cloned.1.call-update) | async-done | bytes 1048592 | tf_op jit(solution)/shard_map/all_gather | solution.py:40
  73.2 6.3 %convolution_convert_fusion = bf16[896,4096]{1,0:T(8,128)(2,1)} fusion(bf16[128,896]{1,0:T(8,128)(2,1)S(1)} %copy-done, bf16[128,4096]{0,1:T(8,128)(2,1)} %all-gather.5.cloned.1.call-done), kind=kOutput, calls=%fused_computation.9 | convolution fusion | flops 943194112 | bytes 8617984 | tf_op jit(solution)/shard_map/tr,td->rd/dot_general | solution.py:52
  79.4 20.9 %reshape.228 = bf16[14,64,64,64]{3,2,1,0:T(8,128)(2,1)} reshape(bf16[896,4096]{1,0:T(8,128)(2,1)} %convolution_convert_fusion) | data formatting | bytes 14680064 | tf_op jit(solution)/shard_map/reshape | solution.py:55
  100.3 16.5 %copy.30 = bf16[14,64,64,64]{3,1,2,0:T(8,128)(2,1)} copy(bf16[14,64,64,64]{3,2,1,0:T(8,128)(2,1)} %reshape.228) | data formatting | bytes 14680064 | tf_op jit(solution)/shard_map/reshape | solution.py:55
  116.9 12.8 %gather_fusion.1 = bf16[512,64,64]{2,1,0:T(8,128)(2,1)} fusion(bf16[14,64,64,64]{3,1,2,0:T(8,128)(2,1)} %copy.30, s32[512]{0:T(512)S(1)} %bitcast.35), kind=kCustom, calls=%fused_computation.1 | custom fusion | bytes 8392704 | tf_op jit(solution)/shard_map/gather | solution.py:55
  129.6 12.1 %reshape.229 = bf16[32,16,4096]{2,1,0:T(8,128)(2,1)} reshape(bf16[512,64,64]{2,1,0:T(8,128)(2,1)} %gather_fusion.1) | data formatting | bytes 8388608 | tf_op jit(solution)/shard_map/reshape | solution.py:58
  141.7 14.6 %all-to-all-start = ((bf16[32,16,4096]{2,1,0:T(8,128)(2,1)}), bf16[32,16,4096]{2,1,0:T(8,128)(2,1)}, u32[]{:S(2)}, u32[]{:S(2)}) async-start(bf16[32,16,4096]{2,1,0:T(8,128)(2,1)} %reshape.229), calls=%async_computation.1 | async-start | bytes 8388608 | tf_op jit(solution)/shard_map/all_to_all | solution.py:59
  158.0 155.8 %all-gather.3.cloned.1.call-done = bf16[1,512,4096]{2,1,0:T(8,128)(2,1)} async-done(((bf16[1,16,4096]{2,1,0:T(8,128)(2,1)}), bf16[1,512,4096]{2,1,0:T(8,128)(2,1)}) %all-gather.3.cloned.1.call-update) | async-done | bytes 4194320 | tf_op jit(solution)/shard_map/all_gather | solution.py:30
  313.8 11.9 %scatter_custom_fusion = bf16[896,4096]{1,0:T(8,128)(2,1)} fusion(s32[512]{0:T(512)S(1)} %bitcast.41, bf16[1,512,4096]{2,1,0:T(8,128)(2,1)} %all-gather.3.cloned.1.call-done, bf16[]{:T(256)} %constant.51.clone.1), kind=kCustom, calls=%fused_computation.12 | custom fusion | bytes 11534338 | tf_op jit(solution)/shard_map/scatter | solution.py:15
  325.7 20.9 %reshape.225 = bf16[14,64,64,64]{3,2,1,0:T(8,128)(2,1)} reshape(bf16[896,4096]{1,0:T(8,128)(2,1)} %scatter_custom_fusion) | data formatting | bytes 14680064 | tf_op jit(solution)/shard_map/reshape | solution.py:17
  346.6 16.5 %copy.26 = bf16[14,64,64,64]{3,2,1,0:T(8,128)(2,1)} copy(bf16[14,64,64,64]{3,1,2,0:T(8,128)(2,1)} %bitcast.34) | data formatting | bytes 14680064 | tf_op jit(solution)/shard_map/transpose | solution.py:17
  363.2 20.0 %reshape.226 = bf16[896,4096]{1,0:T(8,128)(2,1)} reshape(bf16[14,64,64,64]{3,2,1,0:T(8,128)(2,1)} %copy.26) | data formatting | bytes 14680064 | tf_op jit(solution)/shard_map/reshape | solution.py:18
  383.2 6.3 %fusion.4 = bf16[128,4096]{0,1:T(8,128)(2,1)} fusion(bf16[896,4096]{1,0:T(8,128)(2,1)} %reshape.226, bf16[128,896]{1,0:T(8,128)(2,1)S(1)} %copy-done), kind=kOutput, calls=%fused_computation.11 | convolution fusion | flops 940048384 | bytes 8617984 | tf_op jit(solution)/shard_map/dot_general | solution.py:36
  389.6 13.5 %gather_fusion = bf16[512,128,64]{1,2,0:T(8,128)(2,1)} fusion(bf16[128,64,64]{0,2,1:T(8,128)(2,1)S(1)} %bitcast.33, s32[1024]{0:T(1024)S(1)} %pad_clamp_fusion), kind=kCustom, calls=%fused_computation | custom fusion | bytes 16779264 | tf_op jit(solution)/shard_map/jit(_take)/gather | solution.py:45
  403.1 6.5 %copy.28 = bf16[1,512,4096]{1,2,0:T(8,128)(2,1)} copy(bf16[1,512,4096]{2,1,0:T(8,128)(2,1)} %all-gather.3.cloned.1.call-done) | data formatting | bytes 8388608 | tf_op jit(solution)/shard_map/all_gather | solution.py:30
  409.6 12.9 %copy.29 = bf16[512,64,64]{2,1,0:T(8,128)(2,1)} copy(bf16[512,64,64]{0,2,1:T(8,128)(2,1)} %bitcast.36) | data formatting | bytes 8388608 | tf_op jit(solution)/shard_map/reshape;squeeze | solution.py:46
  422.5 14.0 %fusion = f32[512,128,64]{1,2,0:T(8,128)} fusion(bf16[512,64,64]{2,1,0:T(8,128)(2,1)} %copy.29, bf16[512,128,64]{1,2,0:T(8,128)(2,1)} %gather_fusion, pred[512]{0:T(512)(128)(4,1)S(1)} %compare_and_fusion), kind=kOutput, calls=%fused_computation.4 | convolution fusion | flops 541065216 | bytes 29360640 | tf_op jit(solution)/shard_map/tnj,nij->nti/dot_general | solution.py:47
  436.5 52.0 %scatter_fusion = f32[14,128,64]{1,2,0:T(8,128)S(1)} fusion(f32[14,128,64]{1,2,0:T(8,128)S(1)} %broadcast_in_dim.46, s32[512]{0:T(512)S(1)} %bitcast.39, f32[512,128,64]{1,2,0:T(8,128)} %fusion), kind=kCustom, calls=%fused_computation.3 | custom fusion | flops 4194304 | bytes 50333696 | tf_op jit(solution)/shard_map/scatter-add | solution.py:50
  488.6 0.8 copy.32
  489.4 1.6 copy.31
  491.0 2.8 convert_reduce_fusion
  (26 shorter events, 2.8 us)
Async XLA Ops:
  8.0 65.2 %copy-start = (bf16[128,896]{1,0:T(8,128)(2,1)S(1)}, bf16[128,896]{1,0:T(8,128)(2,1)}, u32[]{:S(2)}) copy-start(bf16[128,896]{1,0:T(8,128)(2,1)} %param.5) | copy-start | bytes 688132
  8.0 65.2 %all-gather.5.cloned.1.call-start = ((), (), s32[]{:S(2)}) async-start(), calls=%async_computation.4 | async-start | bytes 1114112 | tf_op jit(solution)/shard_map/all_gather | solution.py:40
  129.6 27.4 %copy-start.3 = (bf16[1,16,4096]{2,1,0:T(8,128)(2,1)S(1)}, bf16[1,16,4096]{2,1,0:T(8,128)(2,1)}, u32[]{:S(2)}) copy-start(bf16[1,16,4096]{2,1,0:T(8,128)(2,1)} %param.7) | copy-start | bytes 393220
  141.7 349.3 %all-to-all-start = ((bf16[32,16,4096]{2,1,0:T(8,128)(2,1)}), bf16[32,16,4096]{2,1,0:T(8,128)(2,1)}, u32[]{:S(2)}, u32[]{:S(2)}) async-start(bf16[32,16,4096]{2,1,0:T(8,128)(2,1)} %reshape.229), calls=%async_computation.1 | async-start | bytes 8388608 | tf_op jit(solution)/shard_map/all_to_all | solution.py:59
  156.3 157.5 %all-gather.3.cloned.1.call-start = ((), (), s32[]{:S(2)}) async-start(), calls=%async_computation.2 | async-start | bytes 4325376 | tf_op jit(solution)/shard_map/all_gather | solution.py:30
  157.8 331.6 %reduce-scatter.2.cloned.1.call-start = ((), (), s32[]{:S(2)}) async-start(), calls=%async_computation.3 | async-start | bytes 1114112 | tf_op jit(solution)/shard_map/reduce_scatter | solution.py:37
  383.2 6.4 %copy-start.2 = (bf16[128,4096]{0,1:T(8,128)(2,1)S(1)}, bf16[128,4096]{0,1:T(8,128)(2,1)}, u32[]{:S(2)}) copy-start(bf16[128,4096]{0,1:T(8,128)(2,1)} %all-gather.5.cloned.1.call-done) | copy-start | bytes 3145732
  436.5 58.1 %copy-start.1 = (bf16[128,896]{1,0:T(8,128)(2,1)S(1)}, bf16[128,896]{1,0:T(8,128)(2,1)}, u32[]{:S(2)}) copy-start(bf16[128,896]{1,0:T(8,128)(2,1)} %param.5) | copy-start | bytes 688132
Sparse Core Ops, SparseCore 0:
  12.4 60.6 all-gather.4
  389.7 83.0 reduce-scatter.1
Sparse Core Ops, SparseCore 1:
  159.5 154.3 all-gather.2
where the time goes:
time: 506 us; the launch traced here: 502 us
  waiting for transfers between devices  194 us (38%)
  local copies, waits for them, and re-layouts  171 us (34%)
  other arithmetic  56.5 us (11%)
  matrix products  26.5 us (5%)
  blocking collectives  22.7 us (4%)
  between operations  16.9 us (3%)
  starting transfers between devices  14.9 us (3%)
    all_gather x1, waiting for transfers between devices, on_device(): lax.all_gather(masked, 'fsdp', axis=1, tiled=True)  156 us
    scatter-add x1, other arithmetic, on_device(): jax.ops.segment_sum(row_terms, piece_index // block_cols, num_segments=bl...  52 us
    all_gather x1, waiting for transfers between devices, on_device(): full_grad = lax.all_gather(grad_out, 'tensor', axis=1, tiled=True)  38 us
    reshape x2, local copies, waits for them, and re-layouts, on_device(): product.reshape(block_rows, BLK, block_cols, BLK)  37.4 us
    squeeze x1, blocking collectives, on_device(): block_index = gathered[1][0]  22.7 us
    reshape x1, local copies, waits for them, and re-layouts, build_window(): block_grid.reshape(block_rows, block_cols, BLK, BLK).transpose(0, 2, 1, 3)  20.9 us
    reshape x1, local copies, waits for them, and re-layouts, build_window(): return block_grid.reshape(block_rows * BLK, block_cols * BLK)  20 us
    transpose x1, local copies, waits for them, and re-layouts, build_window(): block_grid.reshape(block_rows, block_cols, BLK, BLK).transpose(0, 2, 1, 3)  16.5 us
  transfers between devices with their start and end apart: 4, of which 2 were waited for; matrix products, arithmetic and copies ran while one was open for 36% of the time, Pallas kernels for 0%

commit v1 on v0

v1 whole, which is shorter than its diff:
```python
import functools
import math

import jax
import jax.numpy as jnp
from jax import lax
from jax.experimental import pallas as pl
from jax.experimental.pallas import tpu as pltpu
from jax.sharding import PartitionSpec as P

BLK = 64
HALF = BLK // 2
LANES = 2 * BLK
MESH = pl.DeviceIdType.MESH
F32 = jnp.float32
BF16 = jnp.bfloat16
NN = (((1,), (0,)), ((), ()))
NT = (((1,), (1,)), ((), ()))


def dot(a, b, dims=NN):
    return lax.dot_general(a, b, dims, preferred_element_type=F32)


def lane_iota(shape):
    return lax.broadcasted_iota(jnp.int32, shape, 1)


def kernel(
    n_f, n_t,
    hid_ref, grad_ref, w_ref, ids_ref,
    proj_ref, dh_ref, gs_ref,
    wall, ids_all, fg, h2, hm, gd, q, bw,
    g_own, g_oth, g_sib, ring_r, ring_l, send_r, send_l,
    parts, psend, dacc, inv_v, ids_v, inv_s, ids_s,
    ids_ss, ids_rs, gr_ss, gr_rs, wr_ss, wr_rs, wl_ss, wl_rs, wb_ss, wb_rs,
    gs_ss, gs_rs, rr_ss, rr_rs, rl_ss, rl_rs, pp_ss, pp_rs, loc_s,
):
    cap = w_ref.shape[0]
    half = cap // 2
    toks, units = hid_ref.shape
    cols = grad_ref.shape[1]
    brows = units // BLK
    rows = units // 2
    bcols = n_t * cols // BLK
    n_z = n_f // 2
    h = n_z // 2
    empty = n_f * cap

    f = lax.axis_index("fsdp")
    t = lax.axis_index("tensor")
    z, c = f // 2, f % 2

    def chip(offset):
        return lax.rem(z + offset + n_z, n_z)

    right, left, sib = chip(1) * 2 + c, chip(-1) * 2 + c, z * 2 + 1 - c

    def fpeer(i):
        return lax.rem(f + i, n_f)

    def tpeer(i):
        return lax.rem(t + i, n_t)

    def to_f(src, dst, ss, rs, peer):
        return pltpu.make_async_remote_copy(
            src_ref=src, dst_ref=dst, send_sem=ss, recv_sem=rs,
            device_id={"fsdp": peer}, device_id_type=MESH,
        )

    def to_t(src, dst, ss, rs, peer):
        return pltpu.make_async_remote_copy(
            src_ref=src, dst_ref=dst, send_sem=ss, recv_sem=rs,
            device_id={"tensor": peer}, device_id_type=MESH,
        )

    barrier = pltpu.get_barrier_semaphore()

    def greet_f(i, carry):
        pl.semaphore_signal(barrier, inc=1, device_id={"fsdp": fpeer(i)}, device_id_type=MESH)
        return carry

    def greet_t(i, carry):
        pl.semaphore_signal(barrier, inc=1, device_id={"tensor": tpeer(i)}, device_id_type=MESH)
        return carry

    lax.fori_loop(1, n_f, greet_f, 0)
    lax.fori_loop(1, n_t, greet_t, 0)
    pl.semaphore_wait(barrier, n_f + n_t - 2)

    def w_part(zz, cc, lo, size):
        return wall.at[pl.ds((zz * 2 + cc) * cap + lo, size)]

    def w_right(s):
        src = w_ref if s == 0 else w_part(chip(-s), c, 0, cap)
        dst = w_part(chip(-s), c, 0, cap)
        if s == h - 1:
            src = (w_ref if s == 0 else w_part(chip(-s), c, 0, cap)).at[pl.ds(0, half)]
            dst = w_part(chip(-s), c, 0, half)
        return to_f(src, dst, wr_ss.at[s], wr_rs.at[s], right)

    def w_left(s):
        src = w_ref if s == 0 else w_part(chip(s), c, 0, cap)
        dst = w_part(chip(s), c, 0, cap)
        if s == h - 1:
            src = src.at[pl.ds(half, half)]
            dst = w_part(chip(s), c, half, half)
        return to_f(src, dst, wl_ss.at[s], wl_rs.at[s], left)

    def w_arrived_right(a):
        size = half if a == h - 1 else cap
        ref = w_part(chip(-1 - a), c, 0, size)
        return to_f(ref, ref, wr_ss.at[a], wr_rs.at[a], right)

    def w_arrived_left(a):
        lo, size = (half, half) if a == h - 1 else (0, cap)
        ref = w_part(chip(1 + a), c, lo, size)
        return to_f(ref, ref, wl_ss.at[a], wl_rs.at[a], left)

    def w_sib(k, core):
        if k == 0:
            src = w_ref if core is c else w_part(z, core, 0, cap)
            dst = w_part(z, core, 0, cap)
        elif k <= h:
            a = k - 1
            src = dst = w_part(chip(-1 - a), core, 0, half if a == h - 1 else cap)
        else:
            a = k - 1 - h
            lo, size = (half, half) if a == h - 1 else (0, cap)
            src = dst = w_part(chip(1 + a), core, lo, size)
        return to_f(src, dst, wb_ss.at[k], wb_rs.at[k], sib)

    def ids_copy(i):
        return to_f(ids_ref, ids_all.at[f], ids_ss.at[i], ids_rs.at[f], fpeer(i))

    def ids_arrival(i):
        peer = fpeer(i)
        return to_f(ids_all.at[peer], ids_all.at[peer], ids_ss.at[i], ids_rs.at[peer], peer)

    def grad_copy(i):
        return to_t(grad_ref, fg.at[t], gr_ss.at[i], gr_rs.at[t], tpeer(i))

    def grad_arrival(i):
        peer = tpeer(i)
        return to_t(fg.at[peer], fg.at[peer], gr_ss.at[i], gr_rs.at[peer], peer)

    w_right(0).start()
    w_left(0).start()
    w_sib(0, c).start()

    def start_ids(i, carry):
        ids_copy(i).start()
        return carry

    def start_grad(i, carry):
        grad_copy(i).start()
        return carry

    lax.fori_loop(1, n_f, start_ids, 0)
    lax.fori_loop(1, n_t, start_grad, 0)

    wall[pl.ds(f * cap, cap)] = w_ref[...]
    wall[pl.ds(empty, 8)] = jnp.zeros((8, HALF, LANES), BF16)
    ids_all[f] = ids_ref[...]
    fg[t] = grad_ref[...]

    def pick_units(odd, shape, unit_axis):
        unit = lax.broadcasted_iota(jnp.int32, shape, unit_axis)
        out = lax.broadcasted_iota(jnp.int32, shape, 1 - unit_axis)
        return jnp.where(unit == 2 * out + odd, 1.0, 0.0).astype(BF16)

    def split_hidden():
        for lo in range(0, units, 256):
            size = min(256, units - lo)
            chunk = hid_ref[:, lo:lo + size]
            for odd in range(2):
                sel = pick_units(odd, (size // 2, size), 1)
                h2[lo // 2:(lo + size) // 2, odd * toks:(odd + 1) * toks] = dot(sel, chunk, NT).astype(BF16)
                hm[odd * toks:(odd + 1) * toks, lo // 2:(lo + size) // 2] = dot(chunk, sel, NT).astype(BF16)

    def positions():
        def wait_ids(i, carry):
            ids_arrival(i).wait_recv()
            return carry

        lax.fori_loop(1, n_f, wait_ids, 0)
        lane = lane_iota((cap, LANES))
        row = lax.broadcasted_iota(jnp.int32, (cap, LANES), 0)
        groups = -(-brows * bcols // LANES)

        def owner(j, accs):
            x = ids_all[j]
            ids_v[pl.ds(j, 1), :] = jnp.sum(jnp.where(row == lane, x, 0), axis=0, keepdims=True)
            slot = row + j * cap
            return tuple(
                jnp.minimum(acc, jnp.where(x == lane + p * LANES, slot, empty))
                for p, acc in enumerate(accs)
            )

        accs = lax.fori_loop(
            0, n_f, owner, tuple(jnp.full((cap, LANES), empty, jnp.int32) for _ in range(groups))
        )
        for p, acc in enumerate(accs):
            inv_v[p:p + 1, :] = jnp.min(acc, axis=0, keepdims=True)
        one = pltpu.make_async_copy(inv_v, inv_s, loc_s.at[0])
        two = pltpu.make_async_copy(ids_v, ids_s, loc_s.at[1])
        one.start()
        two.start()
        one.wait()
        two.wait()

    def product(u, carry):
        src = fg[u // 2, :, pl.ds(pl.multiple_of(lax.rem(u, 2) * LANES, LANES), LANES)].astype(F32)
        swapped = pltpu.roll(src, BLK, 1)
        low = lane_iota((toks, LANES)) < BLK
        gd[u, 0:toks, 0:LANES] = jnp.where(low, src, 0.0).astype(BF16)
        gd[u, toks:2 * toks, 0:LANES] = jnp.where(low, 0.0, swapped).astype(BF16)
        gd[u, 0:toks, LANES:2 * LANES] = jnp.where(low, swapped, 0.0).astype(BF16)
        gd[u, toks:2 * toks, LANES:2 * LANES] = jnp.where(low, 0.0, src).astype(BF16)
        res = dot(h2[...], gd[u]).astype(BF16)
        for r in range(brows):
            q[r * bcols + 2 * u] = res[r * HALF:(r + 1) * HALF, 0:LANES]
            q[r * bcols + 2 * u + 1] = res[r * HALF:(r + 1) * HALF, LANES:2 * LANES]
        return carry

    def wait_grads():
        def wait_grad(i, carry):
            grad_arrival(i).wait_recv()
            return carry

        lax.fori_loop(1, n_t, wait_grad, 0)

    n_u = 2 * n_t
    for a in range(h):
        w_arrived_right(a).wait_recv()
        if a < h - 1:
            w_right(a + 1).start()
        w_sib(1 + a, c).start()
        w_arrived_left(a).wait_recv()
        if a < h - 1:
            w_left(a + 1).start()
        w_sib(1 + h + a, c).start()
        if a == 0:
            split_hidden()
        if a == min(1, h - 1):
            positions()
        if a == min(3, h - 1):
            wait_grads()
        if h == 8:
            if 3 <= a <= 6:
                lax.fori_loop((a - 3) * n_u // 4, (a - 2) * n_u // 4, product, 0)
        elif a == h - 1:
            lax.fori_loop(0, n_u, product, 0)

    def pick(d):
        def one(i, carry):
            g_own[d, i] = q[ids_s[2 * d + c, i]]
            g_oth[d, i] = q[ids_s[2 * d + 1 - c, i]]
            return carry

        lax.fori_loop(0, cap, one, 0, unroll=4)
        g_copy(d).start()

    def g_copy(d):
        return to_f(g_oth.at[d], g_sib.at[d], gs_ss.at[d], gs_rs.at[d], sib)

    def total(d, lo, size, arrived=None):
        part = pl.ds(lo, size)
        value = g_own[d, part].astype(F32) + g_sib[d, part].astype(F32)
        return value if arrived is None else value + arrived.astype(F32)

    def ring_copy(s, buf, dst, ss, rs, peer, lo):
        part = pl.ds(lo, half if s == 0 else cap)
        return to_f(buf.at[s, part], dst.at[s, part], ss.at[s], rs.at[s], peer)

    def right_copy(s):
        return ring_copy(s, send_r, ring_r, rr_ss, rr_rs, right, 0)

    def left_copy(s):
        return ring_copy(s, send_l, ring_l, rl_ss, rl_rs, left, half if s == 0 else 0)

    def combine(s):
        d = chip(h - s)
        g_copy(d).wait_recv()
        if s == 0:
            send_r[0, 0:half] = total(d, 0, half).astype(BF16)
            right_copy(0).start()
            send_l[0, half:cap] = total(d, half, half).astype(BF16)
            left_copy(0).start()
            return
        right_copy(s - 1).wait_recv()
        if s == 1:
            send_r[1, 0:half] = total(d, 0, half, ring_r[0, 0:half]).astype(BF16)
            send_r[1, half:cap] = total(d, half, half).astype(BF16)
        else:
            send_r[s] = total(d, 0, cap, ring_r[s - 1]).astype(BF16)
        right_copy(s).start()
        d = chip(s - h)
        g_copy(d).wait_recv()
        left_copy(s - 1).wait_recv()
        if s == 1:
            send_l[1, 0:half] = total(d, 0, half).astype(BF16)
            send_l[1, half:cap] = total(d, half, half, ring_l[0, half:cap]).astype(BF16)
        else:
            send_l[s] = total(d, 0, cap, ring_l[s - 1]).astype(BF16)
        left_copy(s).start()

    def part_copy(peer):
        return to_t(psend.at[peer], parts.at[t], pp_ss.at[peer], pp_rs.at[t], peer)

    def columns(i, carry):
        tt = tpeer(i)
        low = lane_iota((toks, LANES)) < BLK
        for v in range(2):
            u = tt * 2 + v
            for r in range(brows):
                for side in range(2):
                    pos = r * bcols + 2 * u + side
                    bw[v, r * HALF:(r + 1) * HALF, side * LANES:(side + 1) * LANES] = wall[
                        inv_s[lax.div(pos, LANES), lax.rem(pos, LANES)]
                    ]
            res = dot(hm[...], bw[v])
            top_a, top_b = res[0:toks, 0:LANES], res[0:toks, LANES:2 * LANES]
            bot_a, bot_b = res[toks:2 * toks, 0:LANES], res[toks:2 * toks, LANES:2 * LANES]
            tile = jnp.where(low, top_a, bot_b) + pltpu.roll(jnp.where(low, top_b, bot_a), BLK, 1)
            psend[tt, :, v * LANES:(v + 1) * LANES] = tile.astype(BF16)
            dacc[...] += dot(gd[u], bw[v], NT)
        return carry

    def columns_and_send(i, carry):
        columns(i, carry)
        part_copy(tpeer(i)).start()
        return carry

    dacc[...] = jnp.zeros_like(dacc)
    pick(chip(h))
    if h > 1:
        pick(chip(h - 1))
        pick(chip(1 - h))
    combine(0)
    for k in range(2 * h + 1):
        w_sib(k, 1 - c).wait_recv()

    for s in range(h):
        if s > 0:
            combine(s)
        if s + 2 < h:
            pick(chip(h - s - 2))
            pick(chip(s + 2 - h))
        elif s + 2 == h or h == 1:
            pick(chip(0))
        lo, hi = s * n_t // h, (s + 1) * n_t // h
        if s == h - 1:
            lax.fori_loop(1 + lo, hi, columns_and_send, 0)
            columns(0, 0)
        else:
            lax.fori_loop(1 + lo, 1 + hi, columns_and_send, 0)

    for lo in range(0, units, 256):
        size = min(256, units - lo)
        even = dacc[0:toks, lo // 2:(lo + size) // 2].astype(BF16)
        odd = dacc[toks:2 * toks, lo // 2:(lo + size) // 2].astype(BF16)
        dh_ref[:, lo:lo + size] = (
            dot(even, pick_units(0, (size // 2, size), 1))
            + dot(odd, pick_units(1, (size // 2, size), 1))
        ).astype(BF16)

    proj_acc = psend[t].astype(F32)
    for i in range(1, n_t):
        peer = tpeer(i)
        to_t(parts.at[peer], parts.at[peer], pp_ss.at[peer], pp_rs.at[peer], peer).wait_recv()
        proj_acc += parts[peer].astype(F32)
    proj_ref[...] = proj_acc.astype(BF16)

    g_copy(z).wait_recv()
    right_copy(h - 1).wait_recv()
    left_copy(h - 1).wait_recv()
    gs_ref[...] = total(z, 0, cap) + ring_r[h - 1].astype(F32) + ring_l[h - 1].astype(F32)

    def sent_f(i, carry):
        ids_copy(i).wait_send()
        return carry

    def sent_t(i, carry):
        grad_copy(i).wait_send()
        part_copy(tpeer(i)).wait_send()
        return carry

    lax.fori_loop(1, n_f, sent_f, 0)
    lax.fori_loop(1, n_t, sent_t, 0)
    for s in range(h):
        w_right(s).wait_send()
        w_left(s).wait_send()
        right_copy(s).wait_send()
        left_copy(s).wait_send()
    for k in range(2 * h + 1):
        w_sib(k, c).wait_send()

    def sent_g(d, carry):
        g_copy(d).wait_send()
        return carry

    lax.fori_loop(0, n_z, sent_g, 0)


def on_device(hidden, grad_out, weight_slots, block_ids, slot_count):
    n_f, n_t = lax.axis_size("fsdp"), lax.axis_size("tensor")
    toks, units = hidden.shape
    cols = grad_out.shape[1]
    cap = weight_slots.shape[1]
    n_z = n_f // 2
    h = n_z // 2
    brows, bcols = units // BLK, n_t * cols // BLK
    live = jnp.arange(cap) < slot_count[0, 0]
    packed = jnp.where(live[:, None], weight_slots[0], 0).reshape(cap, HALF, LANES)
    ids = jnp.broadcast_to(block_ids[0][:, None], (cap, LANES))
    block = (cap, HALF, LANES)
    dma = pltpu.SemaphoreType.DMA
    vmem = pl.BlockSpec(memory_space=pltpu.VMEM)
    groups = -(-brows * bcols // LANES)
    projected, d_hidden, grads = pl.pallas_call(
        functools.partial(kernel, n_f, n_t),
        out_shape=(
            jax.ShapeDtypeStruct((toks, cols), BF16),
            jax.ShapeDtypeStruct((toks, units), BF16),
            jax.ShapeDtypeStruct(block, F32),
        ),
        in_specs=[vmem] * 4,
        out_specs=(vmem, vmem, vmem),
        scratch_shapes=[
            pltpu.VMEM((n_f * cap + 8, HALF, LANES), BF16),
            pltpu.VMEM((n_f, cap, LANES), jnp.int32),
            pltpu.VMEM((n_t, toks, cols), BF16),
            pltpu.VMEM((units // 2, 2 * toks), BF16),
            pltpu.VMEM((2 * toks, units // 2), BF16),
            pltpu.VMEM((2 * n_t, 2 * toks, 2 * LANES), BF16),
            pltpu.VMEM((brows * bcols, HALF, LANES), BF16),
            pltpu.VMEM((2, units // 2, 2 * LANES), BF16),
            pltpu.VMEM((n_z,) + block, BF16),
            pltpu.VMEM((n_z,) + block, BF16),
            pltpu.VMEM((n_z,) + block, BF16),
            pltpu.VMEM((h,) + block, BF16),
            pltpu.VMEM((h,) + block, BF16),
            pltpu.VMEM((h,) + block, BF16),
            pltpu.VMEM((h,) + block, BF16),
            pltpu.VMEM((n_t, toks, cols), BF16),
            pltpu.VMEM((n_t, toks, cols), BF16),
            pltpu.VMEM((2 * toks, units // 2), F32),
            pltpu.VMEM((groups, LANES), jnp.int32),
            pltpu.VMEM((n_f, LANES), jnp.int32),
            pltpu.SMEM((groups, LANES), jnp.int32),
            pltpu.SMEM((n_f, LANES), jnp.int32),
            dma((n_f,)), dma((n_f,)), dma((n_t,)), dma((n_t,)),
            dma((h,)), dma((h,)), dma((h,)), dma((h,)),
            dma((2 * h + 1,)), dma((2 * h + 1,)),
            dma((n_z,)), dma((n_z,)),
            dma((h,)), dma((h,)), dma((h,)), dma((h,)),
            dma((n_t,)), dma((n_t,)), dma((2,)),
        ],
        compiler_params=pltpu.CompilerParams(
            collective_id=0, has_side_effects=True, vmem_limit_bytes=56 * 1024 * 1024
        ),
        cost_estimate=pl.CostEstimate(
            flops=10 * toks * units * n_t * cols, bytes_accessed=2 * 1024 * 1024, transcendentals=0
        ),
    )(hidden, grad_out, packed, ids)
    scale = 1.0 / math.sqrt(toks * n_f)
    flat = grads.reshape(cap, BLK * BLK)
    grad_blocks = jnp.where(live[:, None], flat * scale, jnp.zeros_like(flat))
    return (projected, d_hidden, grad_blocks[None])


def solution(mesh):
    in_specs = (
        P("fsdp", "tensor"),
        P("fsdp", "tensor"),
        P("tensor", "fsdp", None),
        P("tensor", "fsdp"),
        P("tensor", "fsdp"),
    )
    out_specs = (P("fsdp", "tensor"), P("fsdp", "tensor"), P("tensor", "fsdp", None))
    return jax.shard_map(
        on_device, mesh=mesh, in_specs=in_specs, out_specs=out_specs, check_vma=False
    )
```

time: 506 us -> 113 us (0.22)
  the two profiles are of different devices: /device:TPU:33 before, /device:TPU:6 now
where the time goes in v1:
time: 113 us; the launch traced here: 112 us
  Pallas kernels  105 us (93%)
  local copies, waits for them, and re-layouts  3.65 us (3%)
  other arithmetic  2.51 us (2%)
  between operations  1.33 us (1%)
    pallas_call x1, Pallas kernels, on_device(): pl.pallas_call(functools.partial(kernel, n_f, n_t), out_shape=(jax.ShapeD...  105 us
    unnamed x9, local copies, waits for them, and re-layouts  2.93 us

profile of v1, /device:TPU:6, one launch (start us, length us, event | category | flops | bytes accessed | tf_op | source)
XLA Modules:
  0.0 112.3 jit_solution(10828705979613981502)
XLA Ops:
  1.3 0.0 copy-start.2
  1.3 0.6 copy-done.2
  1.9 0.7 broadcast_in_dim.36.ids_ref
  2.6 0.9 copy.8
  3.5 0.7 bitcast_select_fusion.w_ref
  4.3 104.8 %shard_map.76 = (bf16[128,256]{1,0:T(8,128)(2,1)}, bf16[128,896]{1,0:T(8,128)(2,1)}, f32[16,32,128]{2,1,0:T(8,128)}) custom-call(bf16[128,896]{1,0:T(8,128)(2,1)} %hid_ref.1, bf16[128,256]{1,0:T(8,128)(2,1)} %grad_ref.1, bf16[16,32,128]{2,1,0:T(8,128)(2,1)} %bitcast_select_fusion.w_ref, s32[16,128]{1,0:T(8,128)} %broadcast_in_dim.36.ids_ref), custom_call_target="tpu_custom_call" | custom-call | flops 4697620480 | bytes 2097152 | tf_op jit(solution)/shard_map/pallas_call | solution.py:421
  109.1 1.0 broadcast_multiply_fusion
  110.1 0.1 mul.18
  110.2 0.0 copy-start.1
  110.2 0.0 copy-start
  110.2 0.8 broadcast_select_fusion
  111.0 0.0 copy-done.1
  111.0 0.6 copy.12
  111.6 0.0 copy-done
  111.6 0.7 copy.13
  (1 shorter events, 0.0 us)
Async XLA Ops:
  1.3 0.7 copy-start.2
  110.2 0.8 copy-start.1
  110.2 1.5 %copy-start = (bf16[128,896]{1,0:T(8,128)(2,1)S(1)}, bf16[128,896]{1,0:T(8,128)(2,1)}, u32[]{:S(2)}) copy-start(bf16[128,896]{1,0:T(8,128)(2,1)} %get-tuple-element.13) | copy-start | bytes 688132

commit v2 on v1

v2 whole, which is shorter than its diff:
```python
import functools
import math

import jax
import jax.numpy as jnp
from jax import lax
from jax.experimental import pallas as pl
from jax.experimental.pallas import tpu as pltpu
from jax.sharding import PartitionSpec as P

BLK = 64
HALF = BLK // 2
LANES = 2 * BLK
MESH = pl.DeviceIdType.MESH
F32 = jnp.float32
BF16 = jnp.bfloat16
K = 2
NN = (((1,), (0,)), ((), ()))
NT = (((1,), (1,)), ((), ()))


def dot(a, b, dims=NN):
    return lax.dot_general(a, b, dims, preferred_element_type=F32)


def lane_iota(shape):
    return lax.broadcasted_iota(jnp.int32, shape, 1)


def kernel(
    n_f, n_t,
    hid_ref, grad_ref, slots_ref, ids_ref, count_ref,
    proj_ref, dh_ref, gs_ref,
    wall, flat, w_ref, ids_all, fg, h2, hm, gd, q, bw,
    g_own, g_oth, g_sib, ring_r, ring_l, send_r, send_l,
    parts, psend, dacc, inv_v, inv_s, ids_s,
    ids_ss, ids_rs, gr_ss, gr_rs, wr_ss, wr_rs, wl_ss, wl_rs, wb_ss, wb_rs,
    gs_ss, gs_rs, rr_ss, rr_rs, rl_ss, rl_rs, pp_ss, pp_rs, loc_s,
):
    cap = slots_ref.shape[1]
    half, step = cap // 2, cap // K
    toks, units = hid_ref.shape
    cols = grad_ref.shape[1]
    brows = units // BLK
    rows = units // 2
    bcols = n_t * cols // BLK
    n_z = n_f // 2
    h = n_z // 2
    empty = n_f * cap

    f = lax.axis_index("fsdp")
    t = lax.axis_index("tensor")
    z, c = f // 2, f % 2

    def chip(offset):
        return lax.rem(z + offset + n_z, n_z)

    right, left, sib = chip(1) * 2 + c, chip(-1) * 2 + c, z * 2 + 1 - c

    def fpeer(i):
        return lax.rem(f + i, n_f)

    def tpeer(i):
        return lax.rem(t + i, n_t)

    def to_f(src, dst, ss, rs, peer):
        return pltpu.make_async_remote_copy(
            src_ref=src, dst_ref=dst, send_sem=ss, recv_sem=rs,
            device_id={"fsdp": peer}, device_id_type=MESH,
        )

    def to_t(src, dst, ss, rs, peer):
        return pltpu.make_async_remote_copy(
            src_ref=src, dst_ref=dst, send_sem=ss, recv_sem=rs,
            device_id={"tensor": peer}, device_id_type=MESH,
        )

    barrier = pltpu.get_barrier_semaphore()

    def greet_f(i, carry):
        pl.semaphore_signal(barrier, inc=1, device_id={"fsdp": fpeer(i)}, device_id_type=MESH)
        return carry

    def greet_t(i, carry):
        pl.semaphore_signal(barrier, inc=1, device_id={"tensor": tpeer(i)}, device_id_type=MESH)
        return carry

    lax.fori_loop(1, n_f, greet_f, 0)
    lax.fori_loop(1, n_t, greet_t, 0)
    live = lax.broadcasted_iota(jnp.int32, (cap, LANES), 0) < count_ref[0, 0]
    for i in range(HALF):
        piece = slots_ref[0, :, i * LANES:(i + 1) * LANES].astype(F32)
        flat[pl.ds(i, cap, stride=HALF), :] = jnp.where(live, piece, 0.0)
    w_ref[...] = flat[...].reshape(cap, HALF, LANES).astype(BF16)

    def w_part(zz, cc, lo, size):
        return wall.at[pl.ds((zz * 2 + cc) * cap + lo, size)]

    def w_right(s, j):
        dst = w_part(chip(-s), c, j * step, step)
        src = w_ref.at[pl.ds(j * step, step)] if s == 0 else dst
        return to_f(src, dst, wr_ss.at[s, j], wr_rs.at[s, j], right)

    def w_left(s, j):
        dst = w_part(chip(s), c, j * step, step)
        src = w_ref.at[pl.ds(j * step, step)] if s == 0 else dst
        return to_f(src, dst, wl_ss.at[s, j], wl_rs.at[s, j], left)

    def w_arrived_right(a, j):
        ref = w_part(chip(-1 - a), c, j * step, step)
        return to_f(ref, ref, wr_ss.at[a, j], wr_rs.at[a, j], right)

    def w_arrived_left(a, j):
        ref = w_part(chip(1 + a), c, j * step, step)
        return to_f(ref, ref, wl_ss.at[a, j], wl_rs.at[a, j], left)

    def w_sib(k, core):
        if k == 0:
            dst = w_part(z, core, 0, cap)
            src = w_ref if core is c else dst
        elif k <= h:
            a = k - 1
            src = dst = w_part(chip(-1 - a), core, 0, half if a == h - 1 else cap)
        else:
            a = k - 1 - h
            lo, size = (half, half) if a == h - 1 else (0, cap)
            src = dst = w_part(chip(1 + a), core, lo, size)
        return to_f(src, dst, wb_ss.at[k], wb_rs.at[k], sib)

    def ids_copy(i):
        return to_f(ids_ref, ids_all.at[pl.ds(f, 1)], ids_ss.at[i], ids_rs.at[f], fpeer(i))

    def ids_arrival(i):
        peer = fpeer(i)
        ref = ids_all.at[pl.ds(peer, 1)]
        return to_f(ref, ref, ids_ss.at[i], ids_rs.at[peer], peer)

    def grad_copy(i):
        return to_t(grad_ref, fg.at[t], gr_ss.at[i], gr_rs.at[t], tpeer(i))

    def grad_arrival(peer):
        return to_t(fg.at[peer], fg.at[peer], gr_ss.at[0], gr_rs.at[peer], peer)

    def chunks(s):
        return K // 2 if s == h - 1 else K

    def other(j):
        return (j + K // 2) % K

    def start_ids(i, carry):
        ids_copy(i).start()
        return carry

    def start_grad(i, carry):
        grad_copy(i).start()
        return carry

    pl.semaphore_wait(barrier, n_f + n_t - 2)
    lax.fori_loop(1, n_t, start_grad, 0)
    for j in range(chunks(0)):
        w_right(0, j).start()
        w_left(0, other(j)).start()
    w_sib(0, c).start()

    lax.fori_loop(1, n_f, start_ids, 0)

    wall[pl.ds(f * cap, cap)] = w_ref[...]
    wall[pl.ds(empty, 8)] = jnp.zeros((8, HALF, LANES), BF16)
    ids_all[pl.ds(f, 1), :] = ids_ref[...]
    fg[t] = grad_ref[...]

    def pick_units(odd, shape, unit_axis):
        unit = lax.broadcasted_iota(jnp.int32, shape, unit_axis)
        out = lax.broadcasted_iota(jnp.int32, shape, 1 - unit_axis)
        return jnp.where(unit == 2 * out + odd, 1.0, 0.0).astype(BF16)

    def split_hidden():
        for lo in range(0, units, 256):
            size = min(256, units - lo)
            chunk = hid_ref[:, lo:lo + size]
            for odd in range(2):
                sel = pick_units(odd, (size // 2, size), 1)
                h2[lo // 2:(lo + size) // 2, odd * toks:(odd + 1) * toks] = dot(sel, chunk, NT).astype(BF16)
                hm[odd * toks:(odd + 1) * toks, lo // 2:(lo + size) // 2] = dot(chunk, sel, NT).astype(BF16)

    def positions():
        def wait_ids(i, carry):
            ids_arrival(i).wait_recv()
            return carry

        lax.fori_loop(1, n_f, wait_ids, 0)
        lane = lane_iota((cap, LANES))
        diagonal = lane_iota((cap, cap)) == lax.broadcasted_iota(jnp.int32, (cap, cap), 0)
        row = lax.broadcasted_iota(jnp.int32, (cap, LANES), 0)
        groups = -(-brows * bcols // LANES)

        def owner(j, accs):
            x = jnp.sum(jnp.where(diagonal, ids_all[pl.ds(j, 1), :], 0), axis=1, keepdims=True)
            slot = row + j * cap
            return tuple(
                jnp.minimum(acc, jnp.where(x == lane + p * LANES, slot, empty))
                for p, acc in enumerate(accs)
            )

        accs = lax.fori_loop(
            0, n_f, owner, tuple(jnp.full((cap, LANES), empty, jnp.int32) for _ in range(groups))
        )
        for p, acc in enumerate(accs):
            inv_v[p:p + 1, :] = jnp.min(acc, axis=0, keepdims=True)
        one = pltpu.make_async_copy(inv_v, inv_s, loc_s.at[0])
        two = pltpu.make_async_copy(ids_all, ids_s, loc_s.at[1])
        one.start()
        two.start()
        one.wait()
        two.wait()

    def product(i, carry):
        tt = lax.rem(t - i + n_t, n_t)
        low = lane_iota((toks, LANES)) < BLK
        for v in range(2):
            u = 2 * tt + v
            src = fg[tt, :, v * LANES:(v + 1) * LANES].astype(F32)
            swapped = pltpu.roll(src, BLK, 1)
            gd[u, 0:toks, 0:LANES] = jnp.where(low, src, 0.0).astype(BF16)
            gd[u, toks:2 * toks, 0:LANES] = jnp.where(low, 0.0, swapped).astype(BF16)
            gd[u, 0:toks, LANES:2 * LANES] = jnp.where(low, swapped, 0.0).astype(BF16)
            gd[u, toks:2 * toks, LANES:2 * LANES] = jnp.where(low, 0.0, src).astype(BF16)
            res = dot(h2[...], gd[u]).astype(BF16)
            for r in range(brows):
                q[r * bcols + 2 * u] = res[r * HALF:(r + 1) * HALF, 0:LANES]
                q[r * bcols + 2 * u + 1] = res[r * HALF:(r + 1) * HALF, LANES:2 * LANES]
        return carry

    def products(lo, hi):
        if lo == 0 and hi > 0:
            product(0, 0)
            lo = 1

        def arrived(i, carry):
            grad_arrival(lax.rem(t - i + n_t, n_t)).wait_recv()
            return product(i, carry)

        if hi > lo:
            lax.fori_loop(lo, hi, arrived, 0)

    def pick(d):
        def one(i, carry):
            g_own[d, i] = q[ids_s[2 * d + c, i]]
            g_oth[d, i] = q[ids_s[2 * d + 1 - c, i]]
            return carry

        lax.fori_loop(0, cap, one, 0, unroll=4)
        g_copy(d).start()

    def g_copy(d):
        return to_f(g_oth.at[d], g_sib.at[d], gs_ss.at[d], gs_rs.at[d], sib)

    def right_copy(s, j):
        part = pl.ds(j * step, step)
        return to_f(send_r.at[s, part], ring_r.at[s, part], rr_ss.at[s, j], rr_rs.at[s, j], right)

    def left_copy(s, j):
        part = pl.ds(j * step, step)
        return to_f(send_l.at[s, part], ring_l.at[s, part], rl_ss.at[s, j], rl_rs.at[s, j], left)

    def wait_sums(s):
        for d in [chip(h - s)] if s in (0, h) else [chip(h - s), chip(s - h)]:
            g_copy(d).wait_recv()
            g_own[d] = g_own[d] + g_sib[d]

    def combine(s, j):
        arrives = s > 1 or (s == 1 and j < K // 2)
        part = pl.ds(j * step, step)
        if arrives:
            right_copy(s - 1, j).wait_recv()
        value = g_own[chip(h - s), part]
        send_r[s, part] = value + ring_r[s - 1, part] if arrives else value
        right_copy(s, j).start()
        j = other(j)
        part = pl.ds(j * step, step)
        if arrives:
            left_copy(s - 1, j).wait_recv()
        value = g_own[chip(s - h), part]
        send_l[s, part] = value + ring_l[s - 1, part] if arrives else value
        left_copy(s, j).start()

    def part_copy(peer):
        return to_t(psend.at[peer], parts.at[t], pp_ss.at[peer], pp_rs.at[t], peer)

    def part_arrival(peer):
        return to_t(parts.at[peer], parts.at[peer], pp_ss.at[peer], pp_rs.at[peer], peer)

    def columns(i, carry):
        tt = tpeer(i)
        low = lane_iota((toks, LANES)) < BLK
        for v in range(2):
            u = tt * 2 + v
            for r in range(brows):
                for side in range(2):
                    pos = r * bcols + 2 * u + side
                    bw[v, r * HALF:(r + 1) * HALF, side * LANES:(side + 1) * LANES] = wall[
                        inv_s[lax.div(pos, LANES), lax.rem(pos, LANES)]
                    ]
            res = dot(hm[...], bw[v])
            top_a, top_b = res[0:toks, 0:LANES], res[0:toks, LANES:2 * LANES]
            bot_a, bot_b = res[toks:2 * toks, 0:LANES], res[toks:2 * toks, LANES:2 * LANES]
            tile = jnp.where(low, top_a, bot_b) + pltpu.roll(jnp.where(low, top_b, bot_a), BLK, 1)
            psend[tt, :, v * LANES:(v + 1) * LANES] = tile.astype(BF16)
            dacc[...] += dot(gd[u], bw[v], NT)
        return carry

    def columns_and_send(i, carry):
        columns(i, carry)
        part_copy(tpeer(i)).start()
        return carry

    dacc[...] = jnp.zeros_like(dacc)

    def hidden_gradient():
        for lo in range(0, units, 256):
            size = min(256, units - lo)
            even = dacc[0:toks, lo // 2:(lo + size) // 2].astype(BF16)
            odd = dacc[toks:2 * toks, lo // 2:(lo + size) // 2].astype(BF16)
            dh_ref[:, lo:lo + size] = (
                dot(even, pick_units(0, (size // 2, size), 1))
                + dot(odd, pick_units(1, (size // 2, size), 1))
            ).astype(BF16)

    def weights_event(e):
        a, j = events[e]
        w_arrived_right(a, j).wait_recv()
        if a < h - 1 and j < chunks(a + 1):
            w_right(a + 1, j).start()
        w_arrived_left(a, other(j)).wait_recv()
        if a < h - 1 and j < chunks(a + 1):
            w_left(a + 1, other(j)).start()
        if j == chunks(a) - 1:
            w_sib(1 + a, c).start()
            w_sib(1 + h + a, c).start()

    def sums_event(e):
        s, j = hops[e]
        if e == 0:
            wait_sums(0)
        combine(s, j)
        if j == 0 and s + 2 <= h:
            pick(chip(h - s - 2))
            if s + 2 < h:
                pick(chip(s + 2 - h))
        if j == chunks(h - 1 if s == 0 else 0) - 1:
            wait_sums(s + 1)

    events = [(a, j) for a in range(h) for j in range(chunks(a))]
    hops = [(s, j) for s in range(h) for j in range(K // 2 if s == 0 else K)]
    n = len(events)
    first, last = (n + 1) // 4, 2 * n // 3
    for e in range(n):
        weights_event(e)
        if e == 0:
            split_hidden()
        if e == min(2, last - 1):
            positions()
        if first <= e < last:
            products((e - first) * n_t // (last - first), (e + 1 - first) * n_t // (last - first))
        if e == last - 1:
            pick(chip(h))
            pick(chip(h - 1))
            pick(chip(1 - h))
        if e >= last:
            sums_event(e - last)

    for k in range(2 * h + 1):
        w_sib(k, 1 - c).wait_recv()
    begin = n - last
    end = max(begin + 1, n - 2)
    for e in range(begin, n):
        sums_event(e)
        if begin <= e < end:
            lo, hi = (e - begin) * n_t // (end - begin), (e + 1 - begin) * n_t // (end - begin)
            if hi == n_t:
                if hi - 1 > lo:
                    lax.fori_loop(1 + lo, n_t, columns_and_send, 0)
                columns(0, 0)
            elif hi > lo:
                lax.fori_loop(1 + lo, 1 + hi, columns_and_send, 0)
        if e == n - 1:
            hidden_gradient()

    proj_acc = psend[t].astype(F32)
    for i in range(1, n_t):
        peer = tpeer(i)
        part_arrival(peer).wait_recv()
        proj_acc += parts[peer].astype(F32)
    proj_ref[...] = proj_acc.astype(BF16)

    for j in range(K):
        right_copy(h - 1, j).wait_recv()
        left_copy(h - 1, j).wait_recv()
    grads = g_own[z].astype(F32) + ring_r[h - 1].astype(F32) + ring_l[h - 1].astype(F32)
    flat[...] = grads.reshape(cap * HALF, LANES)
    scale = 1.0 / math.sqrt(toks * n_f)
    for i in range(HALF):
        piece = flat[pl.ds(i, cap, stride=HALF), :]
        gs_ref[0, :, i * LANES:(i + 1) * LANES] = jnp.where(live, piece * scale, 0.0)

    def sent_f(i, carry):
        ids_copy(i).wait_send()
        return carry

    def sent_t(i, carry):
        grad_copy(i).wait_send()
        part_copy(tpeer(i)).wait_send()
        return carry

    lax.fori_loop(1, n_f, sent_f, 0)
    lax.fori_loop(1, n_t, sent_t, 0)
    for s, j in events:
        w_right(s, j).wait_send()
        w_left(s, other(j)).wait_send()
    for s, j in hops:
        right_copy(s, j).wait_send()
        left_copy(s, other(j)).wait_send()
    for k in range(2 * h + 1):
        w_sib(k, c).wait_send()

    def sent_g(d, carry):
        g_copy(d).wait_send()
        return carry

    lax.fori_loop(0, n_z, sent_g, 0)


def finish(proj_ref, dh_ref, gs_ref, proj_out, dh_out, gs_out):
    proj_out[...] = proj_ref[...]
    dh_out[...] = dh_ref[...]
    gs_out[...] = gs_ref[...]


def on_device(hidden, grad_out, weight_slots, block_ids, slot_count):
    n_f, n_t = lax.axis_size("fsdp"), lax.axis_size("tensor")
    toks, units = hidden.shape
    cols = grad_out.shape[1]
    cap = weight_slots.shape[1]
    n_z = n_f // 2
    h = n_z // 2
    brows, bcols = units // BLK, n_t * cols // BLK
    block = (cap, HALF, LANES)
    dma = pltpu.SemaphoreType.DMA
    vmem = pl.BlockSpec(memory_space=pltpu.VMEM)
    groups = -(-brows * bcols // LANES)
    projected, d_hidden, grads = pl.pallas_call(
        functools.partial(kernel, n_f, n_t),
        out_shape=(
            jax.ShapeDtypeStruct((toks, cols), BF16),
            jax.ShapeDtypeStruct((toks, units), BF16),
            jax.ShapeDtypeStruct((1, cap, BLK * BLK), F32),
        ),
        in_specs=[vmem] * 4 + [pl.BlockSpec(memory_space=pltpu.SMEM)],
        out_specs=(vmem, vmem, vmem),
        scratch_shapes=[
            pltpu.VMEM((n_f * cap + 8, HALF, LANES), BF16),
            pltpu.VMEM((cap * HALF, LANES), F32),
            pltpu.VMEM(block, BF16),
            pltpu.VMEM((n_f, cap), jnp.int32),
            pltpu.VMEM((n_t, toks, cols), BF16),
            pltpu.VMEM((units // 2, 2 * toks), BF16),
            pltpu.VMEM((2 * toks, units // 2), BF16),
            pltpu.VMEM((2 * n_t, 2 * toks, 2 * LANES), BF16),
            pltpu.VMEM((brows * bcols, HALF, LANES), BF16),
            pltpu.VMEM((2, units // 2, 2 * LANES), BF16),
            pltpu.VMEM((n_z,) + block, BF16),
            pltpu.VMEM((n_z,) + block, BF16),
            pltpu.VMEM((n_z,) + block, BF16),
            pltpu.VMEM((h,) + block, BF16),
            pltpu.VMEM((h,) + block, BF16),
            pltpu.VMEM((h,) + block, BF16),
            pltpu.VMEM((h,) + block, BF16),
            pltpu.VMEM((n_t, toks, cols), BF16),
            pltpu.VMEM((n_t, toks, cols), BF16),
            pltpu.VMEM((2 * toks, units // 2), F32),
            pltpu.VMEM((groups, LANES), jnp.int32),
            pltpu.SMEM((groups, LANES), jnp.int32),
            pltpu.SMEM((n_f, cap), jnp.int32),
            dma((n_f,)), dma((n_f,)), dma((n_t,)), dma((n_t,)),
            dma((h, K)), dma((h, K)), dma((h, K)), dma((h, K)),
            dma((2 * h + 1,)), dma((2 * h + 1,)),
            dma((n_z,)), dma((n_z,)),
            dma((h, K)), dma((h, K)), dma((h, K)), dma((h, K)),
            dma((n_t,)), dma((n_t,)), dma((2,)),
        ],
        compiler_params=pltpu.CompilerParams(
            collective_id=0, has_side_effects=True, vmem_limit_bytes=56 * 1024 * 1024
        ),
        cost_estimate=pl.CostEstimate(
            flops=10 * toks * units * n_t * cols, bytes_accessed=2 * 1024 * 1024, transcendentals=0
        ),
    )(hidden, grad_out, weight_slots, block_ids, slot_count)
    return pl.pallas_call(
        finish,
        out_shape=tuple(jax.ShapeDtypeStruct(x.shape, x.dtype) for x in (projected, d_hidden, grads)),
        in_specs=[vmem] * 3,
        out_specs=(vmem, vmem, vmem),
    )(projected, d_hidden, grads)


def solution(mesh):
    in_specs = (
        P("fsdp", "tensor"),
        P("fsdp", "tensor"),
        P("tensor", "fsdp", None),
        P("tensor", "fsdp"),
        P("tensor", "fsdp"),
    )
    out_specs = (P("fsdp", "tensor"), P("fsdp", "tensor"), P("tensor", "fsdp", None))
    return jax.shard_map(
        on_device, mesh=mesh, in_specs=in_specs, out_specs=out_specs, check_vma=False
    )
```

time: 113 us -> 85.3 us (0.75)
  Pallas kernels: 105 us -> 83.8 us
  local copies, waits for them, and re-layouts: 3.65 us -> 0 us
  other arithmetic: 2.51 us -> 0 us
    pallas_call x1, Pallas kernels: 105 us -> 81.9 us  [on_device(): pl.pallas_call(functools.partial(kernel, n_f, n_t), out_shape=(jax.ShapeD...]
    unnamed x9 -> x0, local copies, waits for them, and re-layouts: 2.93 us -> none
    pallas_call x0 -> x1, Pallas kernels: none -> 1.92 us  [on_device(): pl.pallas_call(finish, out_shape=tuple((jax.ShapeDtypeStruct(x.shape, x.d...]
    select_n x2 -> x0, other arithmetic: 1.53 us -> none  [the longest x1 0.79 us: on_device(): grad_blocks = jnp.where(live[:, None], flat * scale, jnp.zeros_like(flat))]
where the time goes in v2:
time: 85.3 us; the launch traced here: 85.1 us
  Pallas kernels  83.8 us (98%)
  between operations  1.29 us (2%)
    pallas_call x1, Pallas kernels, on_device(): pl.pallas_call(functools.partial(kernel, n_f, n_t), out_shape=(jax.ShapeD...  81.9 us
    pallas_call x1, Pallas kernels, on_device(): pl.pallas_call(finish, out_shape=tuple((jax.ShapeDtypeStruct(x.shape, x.d...  1.92 us

profile of v2, /device:TPU:6, one launch (start us, length us, event | category | flops | bytes accessed | tf_op | source)
XLA Modules:
  0.0 85.1 jit_solution(5925111359478934645)
XLA Ops:
  1.3 81.9 %shard_map.76 = (bf16[128,256]{1,0:T(8,128)(2,1)}, bf16[128,896]{1,0:T(8,128)(2,1)}, f32[1,16,4096]{2,1,0:T(8,128)}) custom-call(bf16[128,896]{1,0:T(8,128)(2,1)} %hid_ref.1, bf16[128,256]{1,0:T(8,128)(2,1)} %grad_ref.1, bf16[1,16,4096]{2,1,0:T(8,128)(2,1)} %slots_ref.1, s32[1,16]{1,0:T(1,128)} %ids_ref.1, s32[1,1]{1,0:T(1,128)S(6)} %copy.8.count_ref), custom_call_target="tpu_custom_call" | custom-call | flops 4697620480 | bytes 2097152 | tf_op jit(solution)/shard_map/pallas_call | solution.py:451
  83.2 1.9 %shard_map.77 = (bf16[128,256]{1,0:T(8,128)(2,1)}, bf16[128,896]{1,0:T(8,128)(2,1)}, f32[1,16,4096]{2,1,0:T(8,128)}) custom-call(bf16[128,256]{1,0:T(8,128)(2,1)} %get-tuple-element.6.proj_ref, bf16[128,896]{1,0:T(8,128)(2,1)} %get-tuple-element.7.dh_ref, f32[1,16,4096]{2,1,0:T(8,128)} %get-tuple-element.8.gs_ref), custom_call_target="tpu_custom_call" | custom-call | tf_op jit(solution)/shard_map/pallas_call | solution.py:498

commit v3 on v2

--- a/solution.py
+++ b/solution.py
@@ -156,12 +156,12 @@
         return carry
 
     pl.semaphore_wait(barrier, n_f + n_t - 2)
-    lax.fori_loop(1, n_t, start_grad, 0)
     for j in range(chunks(0)):
         w_right(0, j).start()
         w_left(0, other(j)).start()
     w_sib(0, c).start()
 
+    lax.fori_loop(1, n_t, start_grad, 0)
     lax.fori_loop(1, n_f, start_ids, 0)
 
     wall[pl.ds(f * cap, cap)] = w_ref[...]
@@ -249,7 +249,7 @@
             g_oth[d, i] = q[ids_s[2 * d + 1 - c, i]]
             return carry
 
-        lax.fori_loop(0, cap, one, 0, unroll=4)
+        lax.fori_loop(0, cap, one, 0, unroll=8)
         g_copy(d).start()
 
     def g_copy(d):
@@ -393,6 +393,31 @@
         proj_acc += parts[peer].astype(F32)
     proj_ref[...] = proj_acc.astype(BF16)
 
+    def sent_f(i, carry):
+        ids_copy(i).wait_send()
+        return carry
+
+    def sent_t(i, carry):
+        grad_copy(i).wait_send()
+        part_copy(tpeer(i)).wait_send()
+        return carry
+
+    def sent_g(d, carry):
+        g_copy(d).wait_send()
+        return carry
+
+    lax.fori_loop(1, n_f, sent_f, 0)
+    lax.fori_loop(1, n_t, sent_t, 0)
+    lax.fori_loop(0, n_z, sent_g, 0)
+    for k in range(2 * h + 1):
+        w_sib(k, c).wait_send()
+    for s, j in events:
+        w_right(s, j).wait_send()
+        w_left(s, other(j)).wait_send()
+    for s, j in hops:
+        right_copy(s, j).wait_send()
+        left_copy(s, other(j)).wait_send()
+
     for j in range(K):
         right_copy(h - 1, j).wait_recv()
         left_copy(h - 1, j).wait_recv()
@@ -402,38 +427,6 @@
     for i in range(HALF):
         piece = flat[pl.ds(i, cap, stride=HALF), :]
         gs_ref[0, :, i * LANES:(i + 1) * LANES] = jnp.where(live, piece * scale, 0.0)
-
-    def sent_f(i, carry):
-        ids_copy(i).wait_send()
-        return carry
-
-    def sent_t(i, carry):
-        grad_copy(i).wait_send()
-        part_copy(tpeer(i)).wait_send()
-        return carry
-
-    lax.fori_loop(1, n_f, sent_f, 0)
-    lax.fori_loop(1, n_t, sent_t, 0)
-    for s, j in events:
-        w_right(s, j).wait_send()
-        w_left(s, other(j)).wait_send()
-    for s, j in hops:
-        right_copy(s, j).wait_send()
-        left_copy(s, other(j)).wait_send()
-    for k in range(2 * h + 1):
-        w_sib(k, c).wait_send()
-
-    def sent_g(d, carry):
-        g_copy(d).wait_send()
-        return carry
-
-    lax.fori_loop(0, n_z, sent_g, 0)
-
-
-def finish(proj_ref, dh_ref, gs_ref, proj_out, dh_out, gs_out):
-    proj_out[...] = proj_ref[...]
-    dh_out[...] = dh_ref[...]
-    gs_out[...] = gs_ref[...]
 
 
 def on_device(hidden, grad_out, weight_slots, block_ids, slot_count):
@@ -451,9 +444,9 @@
     projected, d_hidden, grads = pl.pallas_call(
         functools.partial(kernel, n_f, n_t),
         out_shape=(
-            jax.ShapeDtypeStruct((toks, cols), BF16),
-            jax.ShapeDtypeStruct((toks, units), BF16),
-            jax.ShapeDtypeStruct((1, cap, BLK * BLK), F32),
+            pltpu.VMEM((toks, cols), BF16),
+            pltpu.VMEM((toks, units), BF16),
+            pltpu.VMEM((1, cap, BLK * BLK), F32),
         ),
         in_specs=[vmem] * 4 + [pl.BlockSpec(memory_space=pltpu.SMEM)],
         out_specs=(vmem, vmem, vmem),
@@ -495,12 +488,7 @@
             flops=10 * toks * units * n_t * cols, bytes_accessed=2 * 1024 * 1024, transcendentals=0
         ),
     )(hidden, grad_out, weight_slots, block_ids, slot_count)
-    return pl.pallas_call(
-        finish,
-        out_shape=tuple(jax.ShapeDtypeStruct(x.shape, x.dtype) for x in (projected, d_hidden, grads)),
-        in_specs=[vmem] * 3,
-        out_specs=(vmem, vmem, vmem),
-    )(projected, d_hidden, grads)
+    return (projected, d_hidden, grads)
 
 
 def solution(mesh):

time: 85.3 us -> 84.1 us (0.986)
  Pallas kernels: 83.8 us -> 80.3 us
  local copies, waits for them, and re-layouts: 0 us -> 2.02 us
    pallas_call x2 -> x1, Pallas kernels: 83.8 us -> 80.3 us  [on_device(): pl.pallas_call(functools.partial(kernel, n_f, n_t), out_shape=(pltpu.VMEM...]
    unnamed x0 -> x3, local copies, waits for them, and re-layouts: none -> 2.02 us
where the time goes in v3:
time: 84.1 us; the launch traced here: 83.6 us
  Pallas kernels  80.3 us (95%)
  local copies, waits for them, and re-layouts  2.02 us (2%)
  between operations  1.29 us (2%)
    pallas_call x1, Pallas kernels, on_device(): pl.pallas_call(functools.partial(kernel, n_f, n_t), out_shape=(pltpu.VMEM...  80.3 us
    unnamed x3, local copies, waits for them, and re-layouts  2.02 us

profile of v3, /device:TPU:6, one launch (start us, length us, event | category | flops | bytes accessed | tf_op | source)
XLA Modules:
  0.0 83.6 jit_solution(15911390724570049711)
XLA Ops:
  1.3 80.3 %shard_map.76 = (bf16[128,256]{1,0:T(8,128)(2,1)S(1)}, bf16[128,896]{1,0:T(8,128)(2,1)S(1)}, f32[1,16,4096]{2,1,0:T(8,128)S(1)}) custom-call(bf16[128,896]{1,0:T(8,128)(2,1)} %hid_ref.1, bf16[128,256]{1,0:T(8,128)(2,1)} %grad_ref.1, bf16[1,16,4096]{2,1,0:T(8,128)(2,1)} %slots_ref.1, s32[1,16]{1,0:T(1,128)} %ids_ref.1, s32[1,1]{1,0:T(1,128)S(6)} %copy.14.count_ref), custom_call_target="tpu_custom_call" | custom-call | flops 4697620480 | bytes 2097152 | tf_op jit(solution)/shard_map/pallas_call | solution.py:444
  81.6 0.6 copy.11
  82.2 0.7 copy.12
  82.9 0.7 copy.13

commit v4 on v3

--- a/solution.py
+++ b/solution.py
@@ -244,12 +244,11 @@
             lax.fori_loop(lo, hi, arrived, 0)
 
     def pick(d):
-        def one(i, carry):
-            g_own[d, i] = q[ids_s[2 * d + c, i]]
-            g_oth[d, i] = q[ids_s[2 * d + 1 - c, i]]
-            return carry
-
-        lax.fori_loop(0, cap, one, 0, unroll=8)
+        for core, buf in ((c, g_own), (1 - c, g_oth)):
+            for lo in range(0, cap, 8):
+                blocks = [q[ids_s[2 * d + core, i]] for i in range(lo, lo + 8)]
+                for i, value in enumerate(blocks):
+                    buf[d, lo + i] = value
         g_copy(d).start()
 
     def g_copy(d):
@@ -343,12 +342,12 @@
         if e == 0:
             wait_sums(0)
         combine(s, j)
-        if j == 0 and s + 2 <= h:
-            pick(chip(h - s - 2))
-            if s + 2 < h:
-                pick(chip(s + 2 - h))
         if j == chunks(h - 1 if s == 0 else 0) - 1:
             wait_sums(s + 1)
+            if s + 2 <= h:
+                pick(chip(h - s - 2))
+                if s + 2 < h:
+                    pick(chip(s + 2 - h))
 
     events = [(a, j) for a in range(h) for j in range(chunks(a))]
     hops = [(s, j) for s in range(h) for j in range(K // 2 if s == 0 else K)]

time: 84.1 us -> 84.5 us (level)
  no operation moved by 1% of the time
where the time goes in v4:
time: 84.5 us; the launch traced here: 83.3 us
  Pallas kernels  80 us (95%)
  local copies, waits for them, and re-layouts  2.02 us (2%)
  between operations  1.29 us (2%)
    pallas_call x1, Pallas kernels, on_device(): pl.pallas_call(functools.partial(kernel, n_f, n_t), out_shape=(pltpu.VMEM...  80 us
    unnamed x3, local copies, waits for them, and re-layouts  2.02 us

profile of v4, /device:TPU:6, one launch (start us, length us, event | category | flops | bytes accessed | tf_op | source)
XLA Modules:
  0.0 83.3 jit_solution(7639663069990794999)
XLA Ops:
  1.3 80.0 %shard_map.76 = (bf16[128,256]{1,0:T(8,128)(2,1)S(1)}, bf16[128,896]{1,0:T(8,128)(2,1)S(1)}, f32[1,16,4096]{2,1,0:T(8,128)S(1)}) custom-call(bf16[128,896]{1,0:T(8,128)(2,1)} %hid_ref.1, bf16[128,256]{1,0:T(8,128)(2,1)} %grad_ref.1, bf16[1,16,4096]{2,1,0:T(8,128)(2,1)} %slots_ref.1, s32[1,16]{1,0:T(1,128)} %ids_ref.1, s32[1,1]{1,0:T(1,128)S(6)} %copy.14.count_ref), custom_call_target="tpu_custom_call" | custom-call | flops 4697620480 | bytes 2097152 | tf_op jit(solution)/shard_map/pallas_call | solution.py:443
  81.3 0.6 copy.11
  81.9 0.7 copy.12
  82.6 0.7 copy.13
